TPU v7x, 32 devices: a whole 2x2x4 slice. The times are simulated.
32 devices in a mesh: group: 4 (over x, core), fsdp: 8 (over z, y).
Axes of the slice: x: 2, y: 2, z: 4, core: 2. Of those that a mesh axis runs over, the one named last changes fastest.
Arguments:
- tokens: bfloat16 [16384, 3072], P(('group', 'fsdp')), may hold values from -6 to 6
- student: float32 [4, 3072, 6144], P('group', 'fsdp'), may hold values from -6 to 6
- teacher: float32 [3072, 6144], P('fsdp', 'group'), may hold values from -6 to 6
- norm_gain: float32 [3072], replicated, may hold values from 0.5 to 1.5
- query_gain: float32 [128], replicated, may hold values from 0.5 to 1.5
- key_gain: float32 [128], replicated, may hold values from 0.5 to 1.5
Outputs:
- teacher_new: float32 [3072, 6144], P('fsdp', 'group')
- student_new: float32 [3072, 6144], P('fsdp', 'group')
- query: bfloat16 [16384, 3072], P(('group', 'fsdp'))
- key: bfloat16 [16384, 3072], P(('group', 'fsdp'))
All inputs are finite; a program needn't handle non-finite values.
Results may differ from a plain program's by a relative error of at most 0.0058.
Values may be sent and summed in bfloat16 or wider, within the bound.
A program may use at most 192 MiB of HBM per device.

v0:
```python
import jax
import jax.numpy as jnp
from jax import lax
from jax.sharding import PartitionSpec as P

HEAD = 128


ema_decay = 0.99


def head_norm(values, gain, model_width):
    shaped = values.reshape(values.shape[0], model_width // HEAD, HEAD)
    scaled = shaped * lax.rsqrt(jnp.mean(shaped * shaped, axis=-1, keepdims=True) + 1e-06) * gain
    return scaled.reshape(values.shape[0], model_width).astype(jnp.bfloat16)


def shards(tokens, student, teacher, norm_gain, query_gain, key_gain):
    model_width = tokens.shape[1]
    groups = lax.axis_size("group")
    local_part = student[0]
    wide = tokens.astype(jnp.float32)
    normed = (
        wide * lax.rsqrt(jnp.mean(wide * wide, axis=-1, keepdims=True) + 1e-06) * norm_gain
    ).astype(jnp.bfloat16)
    owned = lax.psum_scatter(local_part, "group", scatter_dimension=1, tiled=True) / groups
    copied = owned.astype(jnp.bfloat16)
    whole_rows = lax.all_gather(copied, "group", axis=1, tiled=True)
    projected = jnp.dot(
        normed,
        lax.all_gather(whole_rows, "fsdp", axis=0, tiled=True),
        preferred_element_type=jnp.float32,
    )
    teacher_new = ema_decay * teacher + (1.0 - ema_decay) * owned
    projected = projected * model_width ** (-0.5)
    query = head_norm(projected[:, :model_width], query_gain, model_width)
    key_out = head_norm(projected[:, model_width:], key_gain, model_width)
    return (teacher_new, owned, query, key_out)


def solution(mesh):
    placed = (
        P(("group", "fsdp"), None),
        P("group", "fsdp", None),
        P("fsdp", "group"),
        P(),
        P(),
        P(),
    )
    return jax.shard_map(
        shards,
        mesh=mesh,
        in_specs=placed,
        out_specs=(
            P("fsdp", "group"),
            P("fsdp", "group"),
            P(("group", "fsdp"), None),
            P(("group", "fsdp"), None),
        ),
        check_vma=False,
    )
```

profile of v0, /device:TPU:0, one launch (start us, length us, event | category | flops | bytes accessed | tf_op | source)
XLA Modules:
  0.0 928.3 jit_solution(1791266310622899166)
XLA Ops:
  7.2 0.0 reduce-scatter.2.cloned.1.call-start
  7.2 0.7 reduce-scatter.2.cloned.1.call-update
  7.9 0.0 copy-start
  7.9 0.0 all-gather.3.cloned.1.call-start
  8.0 83.8 %reduce-scatter.2.cloned.1.call-done = f32[384,1536]{1,0:T(8,128)} async-done(((f32[384,6144]{1,0:T(8,128)}), f32[384,1536]{1,0:T(8,128)}) %reduce-scatter.2.cloned.1.call-update) | async-done | bytes 2359312 | tf_op jit(solution)/shard_map/reduce_scatter | solution.py:26
  91.7 5.3 fusion.10
  97.1 0.0 copy-start.1
  97.1 0.0 copy-start.2
  97.1 0.0 copy-start.3
  97.1 0.0 all-gather.3.cloned.1.call-update
  97.1 0.0 all-gather.5.cloned.1.call-start
  97.2 37.6 %all-gather.3.cloned.1.call-done = bf16[384,6144]{1,0:T(8,128)(2,1)} async-done(((bf16[384,1536]{1,0:T(8,128)(2,1)}), bf16[384,6144]{1,0:T(8,128)(2,1)}) %all-gather.3.cloned.1.call-update) | async-done | bytes 4718608 | tf_op jit(solution)/shard_map/all_gather | solution.py:28
  134.7 0.0 all-gather.5.cloned.1.call-update
  134.8 0.0 copy-done
  134.8 0.7 fusion
  135.5 0.0 copy-done.1
  135.5 0.0 copy-done.2
  135.5 717.2 %all-gather.5.cloned.1.call-done = bf16[3072,6144]{1,0:T(8,128)(2,1)} async-done(((bf16[384,6144]{1,0:T(8,128)(2,1)}), bf16[3072,6144]{1,0:T(8,128)(2,1)}) %all-gather.5.cloned.1.call-update) | async-done | bytes 37748752 | tf_op jit(solution)/shard_map/all_gather | solution.py:31
  852.7 0.0 copy-done.3
  852.7 26.7 %convolution_multiply_fusion = f32[512,6144]{1,0:T(8,128)} fusion(bf16[3072,6144]{1,0:T(8,128)(2,1)} %all-gather.5.cloned.1.call-done, bf16[512,3072]{1,0:T(8,128)(2,1)S(1)} %copy-done, f32[3072]{0:T(1024)S(1)} %copy-done.3, f32[512]{0:T(512)S(1)} %add_rsqrt_fusion.2), kind=kOutput, calls=%fused_computation | convolution fusion | flops 19336790016 | bytes 53491712 | tf_op jit(solution)/shard_map/dot_general | solution.py:29
  879.5 9.0 multiply_bitcast_fusion
  888.5 4.0 copy.18
  892.5 4.5 reduce_sum.29
  897.0 0.1 copy.14
  897.1 0.1 copy.15
  897.3 6.8 copy.16
  904.1 4.5 reduce_sum.28
  908.6 0.1 copy.12
  908.7 0.1 copy.13
  908.8 2.0 mul.119
  910.8 1.8 mul.110
  912.6 9.2 fusion.4
  (4 shorter events, 0.1 us)
Async XLA Ops:
  7.2 84.6 %reduce-scatter.2.cloned.1.call-start = ((), (), s32[]{:S(2)}) async-start(), calls=%async_computation.1 | async-start | bytes 11796480 | tf_op jit(solution)/shard_map/reduce_scatter | solution.py:26
  7.9 126.9 %copy-start = (bf16[512,3072]{1,0:T(8,128)(2,1)S(1)}, bf16[512,3072]{1,0:T(8,128)(2,1)}, u32[]{:S(2)}) copy-start(bf16[512,3072]{1,0:T(8,128)(2,1)} %param.6) | copy-start | bytes 9437188
  7.9 126.8 %all-gather.3.cloned.1.call-start = ((), (), s32[]{:S(2)}) async-start(), calls=%async_computation.2 | async-start | bytes 5898240 | tf_op jit(solution)/shard_map/all_gather | solution.py:28
  97.1 38.4 %copy-start.1 = (f32[128]{0:T(128)S(1)}, f32[128]{0:T(128)}, u32[]{:S(2)}) copy-start(f32[128]{0:T(128)} %param.11) | copy-start | bytes 1540
  97.1 38.4 %copy-start.2 = (f32[128]{0:T(128)S(1)}, f32[128]{0:T(128)}, u32[]{:S(2)}) copy-start(f32[128]{0:T(128)} %param.10) | copy-start | bytes 1540
  97.1 755.6 %copy-start.3 = (f32[3072]{0:T(1024)S(1)}, f32[3072]{0:T(1024)}, u32[]{:S(2)}) copy-start(f32[3072]{0:T(1024)} %param.9) | copy-start | bytes 36868
  97.1 755.6 %all-gather.5.cloned.1.call-start = ((), (), s32[]{:S(2)}) async-start(), calls=%async_computation.3 | async-start | bytes 42467328 | tf_op jit(solution)/shard_map/all_gather | solution.py:31
Sparse Core Ops, SparseCore 0:
  10.6 81.1 reduce-scatter.1
  97.2 37.4 all-gather.2
  136.3 716.3 all-gather.4
where the time goes:
time: 929 us; the launch traced here: 928 us
  waiting for transfers between devices  839 us (90%)
  other arithmetic  33.3 us (4%)
  matrix products  26.7 us (3%)
  local copies, waits for them, and re-layouts  15 us (2%)
  between operations  13.8 us (1%)
    all_gather x1, waiting for transfers between devices, shards(): lax.all_gather(whole_rows, 'fsdp', axis=0, tiled=True)  717 us
    reduce_scatter x1, waiting for transfers between devices, shards(): lax.psum_scatter(local_part, 'group', scatter_dimension=1, tiled=True)  83.8 us
    all_gather x1, waiting for transfers between devices, shards(): whole_rows = lax.all_gather(copied, 'group', axis=1, tiled=True)  37.6 us
    dot_general x1, matrix products, shards(): jnp.dot(normed, lax.all_gather(whole_rows, 'fsdp', axis=0, tiled=True), p...  26.7 us
  transfers between devices with their start and end apart: 3, of which 3 were waited for; matrix products, arithmetic and copies ran while one was open for 0% of the time, Pallas kernels for 0%

commit v1 on v0

v1 whole, which is shorter than its diff:
```python
import functools

import jax
import jax.numpy as jnp
from jax import lax
from jax.experimental import pallas as pl
from jax.experimental.pallas import tpu as pltpu
from jax.sharding import PartitionSpec as P

HEAD = 128
PAIR = 2
EMA_DECAY = 0.99
MESH = pl.DeviceIdType.MESH
ROUTES = ("yx", "xy", "xy")


def chunk_count(width, line):
    heads = width // HEAD
    most = max(1, 24 // line)
    return max(n for n in range(1, heads + 1) if heads % n == 0 and n <= most)


def kernel(
    groups,
    line,
    chunks,
    student,
    tokens,
    teacher,
    norm_gain,
    query_gain,
    key_gain,
    teacher_new,
    student_new,
    query,
    key,
    own_part,
    core_part,
    pair_out,
    pair_in,
    weights,
    normed,
    staged,
    mean_out,
    teacher_out,
    load_sem,
    core_send,
    core_recv,
    pair_send,
    pair_recv,
    line_send,
    line_recv,
    first_send,
    first_recv,
    last_send,
    last_recv,
    token_sem,
    store_sem,
    keep_sem,
    give_send,
    give_recv,
):
    g = lax.axis_index("group")
    f = lax.axis_index("fsdp")
    x, c = g // PAIR, g % PAIR
    z, y = f // PAIR, f % PAIR
    rows, block = mean_out.shape[1], mean_out.shape[2]
    width = block * chunks
    per_token, model_width = tokens.shape
    mate = (x * PAIR + 1 - c, f)
    across = ((1 - x) * PAIR + c, f)
    beside = (g, z * PAIR + 1 - y)
    below = (g, (z - 1) * PAIR + y)
    above = (g, (z + 1) * PAIR + y)

    barrier = pltpu.get_barrier_semaphore()
    for device in (mate, across, beside):
        pl.semaphore_signal(barrier, inc=1, device_id=device, device_id_type=MESH)

    @pl.when(z > 0)
    def _():
        pl.semaphore_signal(barrier, inc=1, device_id=below, device_id_type=MESH)

    @pl.when(z < line - 1)
    def _():
        pl.semaphore_signal(barrier, inc=1, device_id=above, device_id_type=MESH)

    peers = 3 + jnp.where(z > 0, 1, 0) + jnp.where(z < line - 1, 1, 0)
    pl.semaphore_wait(barrier, peers)

    def remote(src, dst, send, recv, device):
        return pltpu.make_async_remote_copy(
            src_ref=src, dst_ref=dst, send_sem=send, recv_sem=recv, device_id=device, device_id_type=MESH
        )

    def columns(half, core, k):
        start = half * (PAIR * width) + core * width + k * block
        return pl.ds(pl.multiple_of(start, HEAD), block)

    def load(k, half):
        return pltpu.make_async_copy(
            student.at[0, :, columns(half, c, k)], own_part.at[k, half], load_sem.at[k, half]
        )

    def to_mate(k, half):
        return remote(
            student.at[0, :, columns(half, 1 - c, k)],
            core_part.at[k, half],
            core_send.at[k, half],
            core_recv.at[k, half],
            mate,
        )

    def to_across(k):
        return remote(pair_out.at[k], pair_in.at[k], pair_send.at[k], pair_recv.at[k], across)

    def shard(k, half, index, count=1):
        span = pl.ds(pl.multiple_of(index * rows, 16), count * rows)
        return weights.at[k, half, span, :]

    def along(k, slab, way):
        part = shard(k, x, slab * PAIR + y)
        return remote(
            part, part, line_send.at[k, way, slab], line_recv.at[k, slab], (below, above)[way]
        )

    def first(k, slab):
        part = shard(k, x, slab * PAIR + y)
        device = across if ROUTES[k % len(ROUTES)] == "xy" else beside
        return remote(part, part, first_send.at[k, slab], first_recv.at[k, slab], device)

    def last(k, slab):
        if ROUTES[k % len(ROUTES)] == "xy":
            span = pl.ds(pl.multiple_of((slab * PAIR + y) * rows, 16), rows)
            part, device = weights.at[k, :, span, :], beside
        else:
            part, device = shard(k, x, slab * PAIR, PAIR), across
        return remote(part, part, last_send.at[k, slab], last_recv.at[k, slab], device)

    def tokens_to_mate():
        return remote(normed.at[c], normed.at[c], token_sem.at[0], token_sem.at[1], mate)

    def stores(k):
        here = pl.ds(k * block, block)
        return (
            pltpu.make_async_copy(mean_out.at[k], student_new.at[:, here], store_sem.at[k, 0]),
            pltpu.make_async_copy(teacher_out.at[k], teacher_new.at[:, here], store_sem.at[k, 1]),
        )

    def out_columns(k):
        return pl.ds(pl.multiple_of(c * width + k * block, HEAD), block)

    def keep(k, half):
        out = (query, key)[half]
        return pltpu.make_async_copy(
            staged.at[k, half, c], out.at[:, out_columns(k)], keep_sem.at[k, half]
        )

    def give(k, half):
        out = (query, key)[half]
        return remote(
            staged.at[k, half, 1 - c],
            out.at[:, out_columns(k)],
            give_send.at[k, half],
            give_recv.at[k, half],
            mate,
        )

    def norm_tokens():
        step = 64

        def body(i, carry):
            at = pl.ds(pl.multiple_of(i * step, step), step)
            wide = tokens[at, :].astype(jnp.float32)
            scale = lax.rsqrt(jnp.mean(wide * wide, axis=-1, keepdims=True) + 1e-06)
            normed[c, at, :] = (wide * scale * norm_gain[...]).astype(jnp.bfloat16)
            return carry

        lax.fori_loop(0, per_token // step, body, 0)
        tokens_to_mate().start()

    def sum_cores(k):
        for half in range(PAIR):
            load(k, half).wait()
            to_mate(k, half).wait_recv()
        pair_out[k] = (own_part[k, 1 - x] + core_part[k, 1 - x]).astype(jnp.bfloat16)
        to_across(k).start()

    def sum_pair(k):
        to_across(k).wait_recv()
        total = (own_part[k, x] + core_part[k, x] + pair_in[k].astype(jnp.float32)) / groups
        mean_out[k] = total
        here = pl.ds(k * block, block)
        teacher_out[k] = EMA_DECAY * teacher[:, here] + (1.0 - EMA_DECAY) * total
        weights[k, x, pl.ds(pl.multiple_of(f * rows, 16), rows), :] = total.astype(jnp.bfloat16)

        @pl.when(z > 0)
        def _():
            along(k, z, 0).start()

        @pl.when(z < line - 1)
        def _():
            along(k, z, 1).start()

        first(k, z).start()
        for copy in stores(k):
            copy.start()

    def sides(t):
        yield z >= t, z - t, 1, z < line - 1
        yield z < line - t, z + t, 0, z > 0

    def line_step(k, t):
        for there, slab, way, onward in sides(t):

            @pl.when(there)
            def _():
                along(k, slab, way).wait_recv()

                @pl.when(onward)
                def _():
                    along(k, slab, way).start()

                first(k, slab).start()

    def plane_step(k, t):
        if t == 0:
            first(k, z).wait_recv()
            last(k, z).start()
            return
        for there, slab, way, onward in sides(t):

            @pl.when(there)
            def _():
                first(k, slab).wait_recv()
                last(k, slab).start()

    def arrived(k):
        for slab in range(line):
            last(k, slab).wait_recv()

    def project(k, half, core):
        step = 256 if per_token % 256 == 0 else per_token
        tile = 256 if block % 256 == 0 else HEAD
        gain = (query_gain, key_gain)[half][...]

        def body(i, carry):
            at = pl.ds(pl.multiple_of(i * step, step), step)
            for start in range(0, block, tile):
                made = jnp.dot(
                    normed[core, at, :],
                    weights[k, half, :, start : start + tile],
                    preferred_element_type=jnp.float32,
                )
                made = made * model_width ** (-0.5)
                for head in range(0, tile, HEAD):
                    one = made[:, head : head + HEAD]
                    scale = lax.rsqrt(jnp.mean(one * one, axis=-1, keepdims=True) + 1e-06)
                    staged[k, half, core, at, start + head : start + head + HEAD] = (
                        one * scale * gain
                    ).astype(jnp.bfloat16)
            return carry

        lax.fori_loop(0, per_token // step, body, 0)

    def project_other(k, half):
        project(k, half, 1 - c)
        give(k, half).start()

    def project_own(k, half):
        project(k, half, c)
        keep(k, half).start()

    for k in range(chunks):
        for half in range(PAIR):
            to_mate(k, half).start()
            load(k, half).start()
    norm_tokens()

    events = []
    period, hop = 25, 4
    for k in range(chunks):
        events.append((4 + k, functools.partial(sum_cores, k)))
        events.append((12 + 4 * k, functools.partial(sum_pair, k)))
        for t in range(1, line):
            events.append((12 + 12 * k + hop * t, functools.partial(line_step, k, t)))
        for t in range(line):
            events.append((20 + period * k + 6 * t, functools.partial(plane_step, k, t)))
        done = 30 + period * (k + 1)
        events.append((done, functools.partial(arrived, k)))
        if k == 0:
            events.append((done, lambda: tokens_to_mate().wait_recv()))
        for half in range(PAIR):
            events.append((done + 6 * half, functools.partial(project_other, k, half)))
            events.append((done + 6 * half + 3, functools.partial(project_own, k, half)))
    for _, event in sorted(events, key=lambda item: item[0]):
        event()

    tokens_to_mate().wait_send()
    for k in range(chunks):
        to_across(k).wait_send()
        for half in range(PAIR):
            to_mate(k, half).wait_send()
            keep(k, half).wait()
            give(k, half).wait_send()
        for copy in stores(k):
            copy.wait()
        for slab in range(line):
            first(k, slab).wait_send()
            last(k, slab).wait_send()

            @pl.when((z > 0) & (z <= slab))
            def _():
                along(k, slab, 0).wait_send()

            @pl.when((z < line - 1) & (z >= slab))
            def _():
                along(k, slab, 1).wait_send()

    for k in range(chunks):
        for half in range(PAIR):
            give(k, half).wait_recv()


def shards(groups, members, tokens, student, teacher, norm_gain, query_gain, key_gain):
    per_token, model_width = tokens.shape
    rows, width = teacher.shape
    line = members // PAIR
    chunks = chunk_count(width, line)
    block = width // chunks
    dma = pltpu.SemaphoreType.DMA
    vmem = pl.BlockSpec(memory_space=pltpu.VMEM)
    hbm = pl.BlockSpec(memory_space=pl.ANY)
    f32, bf16 = jnp.float32, jnp.bfloat16
    return pl.pallas_call(
        functools.partial(kernel, groups, line, chunks),
        out_shape=(
            jax.ShapeDtypeStruct((rows, width), f32),
            jax.ShapeDtypeStruct((rows, width), f32),
            jax.ShapeDtypeStruct((per_token, model_width), bf16),
            jax.ShapeDtypeStruct((per_token, model_width), bf16),
        ),
        in_specs=[hbm, vmem, vmem, vmem, vmem, vmem],
        out_specs=(hbm, hbm, hbm, hbm),
        scratch_shapes=[
            pltpu.VMEM((chunks, PAIR, rows, block), f32),
            pltpu.VMEM((chunks, PAIR, rows, block), f32),
            pltpu.VMEM((chunks, rows, block), bf16),
            pltpu.VMEM((chunks, rows, block), bf16),
            pltpu.VMEM((chunks, PAIR, rows * members, block), bf16),
            pltpu.VMEM((PAIR, per_token, model_width), bf16),
            pltpu.VMEM((chunks, PAIR, PAIR, per_token, block), bf16),
            pltpu.VMEM((chunks, rows, block), f32),
            pltpu.VMEM((chunks, rows, block), f32),
            dma((chunks, PAIR)),
            dma((chunks, PAIR)),
            dma((chunks, PAIR)),
            dma((chunks,)),
            dma((chunks,)),
            dma((chunks, 2, line)),
            dma((chunks, line)),
            dma((chunks, line)),
            dma((chunks, line)),
            dma((chunks, line)),
            dma((chunks, line)),
            dma((2,)),
            dma((chunks, 2)),
            dma((chunks, PAIR)),
            dma((chunks, PAIR)),
            dma((chunks, PAIR)),
        ],
        compiler_params=pltpu.CompilerParams(
            collective_id=0, has_side_effects=True, vmem_limit_bytes=60 * 2**20
        ),
        cost_estimate=pl.CostEstimate(
            flops=4 * per_token * model_width * model_width,
            bytes_accessed=4 * student.size + 8 * tokens.size,
            transcendentals=0,
        ),
    )(
        student,
        tokens,
        teacher,
        norm_gain.reshape(1, -1),
        query_gain.reshape(1, -1),
        key_gain.reshape(1, -1),
    )


def solution(mesh):
    placed = (
        P(("group", "fsdp"), None),
        P("group", "fsdp", None),
        P("fsdp", "group"),
        P(),
        P(),
        P(),
    )
    return jax.shard_map(
        functools.partial(shards, mesh.shape["group"], mesh.shape["fsdp"]),
        mesh=mesh,
        in_specs=placed,
        out_specs=(
            P("fsdp", "group"),
            P("fsdp", "group"),
            P(("group", "fsdp"), None),
            P(("group", "fsdp"), None),
        ),
        check_vma=False,
    )
```

time: 929 us -> 256 us (0.28)
  waiting for transfers between devices: 839 us -> 0 us
  Pallas kernels: 0 us -> 245 us
  other arithmetic: 33.3 us -> 0 us
  matrix products: 26.7 us -> 0 us
  between operations: 13.8 us -> 0.65 us
    all_gather x2 -> x0, waiting for transfers between devices: 755 us -> none  [the longest x1 717 us: shards(): lax.all_gather(whole_rows, 'fsdp', axis=0, tiled=True)]
    pallas_call x0 -> x1, Pallas kernels: none -> 245 us  [shards(): pl.pallas_call(functools.partial(kernel, groups, line, chunks), out_shape...]
    reduce_scatter x1 -> x0, waiting for transfers between devices: 83.8 us -> none  [shards(): lax.psum_scatter(local_part, 'group', scatter_dimension=1, tiled=True)]
    dot_general x1 -> x0, matrix products: 26.7 us -> none  [shards(): jnp.dot(normed, lax.all_gather(whole_rows, 'fsdp', axis=0, tiled=True), p...]
    convert_element_type x2 -> x0, other arithmetic: 14.6 us -> none  [the longest x1 9.22 us: head_norm(): return scaled.reshape(values.shape[0], model_width).astype(jnp.bfloat16)]
    reduce_sum x3 -> x0, other arithmetic: 9.67 us -> none  [the longest x2 8.98 us: head_norm(): jnp.mean(shaped * shaped, axis=-1, keepdims=True) + 1e-06]
  transfers between devices with their start and end apart: 3 -> 0, of which waited for: 3 -> 0; matrix products, arithmetic and copies ran while one was open for 0% -> 0% of each run, Pallas kernels for 0% -> 0%
where the time goes in v1:
time: 256 us
  Pallas kernels  245 us (96%)
  local copies, waits for them, and re-layouts  10.8 us (4%)
    pallas_call x1, Pallas kernels, shards(): pl.pallas_call(functools.partial(kernel, groups, line, chunks), out_shape...  245 us
    unnamed x10, local copies, waits for them, and re-layouts  10.8 us

profile of v1, /device:TPU:0, one launch (start us, length us, event | category | flops | bytes accessed | tf_op | source)
XLA Modules:
  0.0 256.0 jit_solution(5188495620129106826)
XLA Ops:
  0.6 244.5 %shard_map.93 = (f32[384,1536]{1,0:T(8,128)}, f32[384,1536]{1,0:T(8,128)}, bf16[512,3072]{1,0:T(8,128)(2,1)}, bf16[512,3072]{1,0:T(8,128)(2,1)}) custom-call(f32[1,384,6144]{2,1,0:T(8,128)} %student.1, bf16[512,3072]{1,0:T(8,128)(2,1)} %tokens.1, f32[384,1536]{1,0:T(8,128)} %teacher.1, f32[1,3072]{1,0:T(1,128)} %bitcast.3, f32[1,128]{1,0:T(1,128)} %bitcast.4, ...), custom_call_target="tpu_custom_call" | custom-call | flops 19327352832 | bytes 22020096 | tf_op jit(solution)/shard_map/pallas_call | solution.py:335
  245.2 0.0 copy-start.2
  245.2 3.4 %copy.14 = f32[384,1536]{1,0:T(8,128)} copy(f32[384,1536]{1,0:T(8,128)} %get-tuple-element.8) | data formatting | bytes 4718592
  248.6 0.0 copy-done.2
  248.6 0.0 copy-start.1
  248.6 1.4 copy.15
  250.0 1.3 copy-done.1
  251.3 0.0 copy-start
  251.3 1.7 copy.16
  253.0 1.4 copy-done
  254.3 1.7 copy.17
Async XLA Ops:
  245.2 3.4 %copy-start.2 = (f32[384,1536]{1,0:T(8,128)S(1)}, f32[384,1536]{1,0:T(8,128)}, u32[]{:S(2)}) copy-start(f32[384,1536]{1,0:T(8,128)} %get-tuple-element.9) | copy-start | bytes 7077892
  248.6 2.7 %copy-start.1 = (bf16[512,3072]{1,0:T(8,128)(2,1)S(1)}, bf16[512,3072]{1,0:T(8,128)(2,1)}, u32[]{:S(2)}) copy-start(bf16[512,3072]{1,0:T(8,128)(2,1)} %get-tuple-element.10) | copy-start | bytes 9437188
  251.3 3.0 %copy-start = (bf16[512,3072]{1,0:T(8,128)(2,1)S(1)}, bf16[512,3072]{1,0:T(8,128)(2,1)}, u32[]{:S(2)}) copy-start(bf16[512,3072]{1,0:T(8,128)(2,1)} %get-tuple-element.11) | copy-start | bytes 9437188

commit v2 on v1

--- a/solution.py
+++ b/solution.py
@@ -286,7 +286,7 @@
             events.append((12 + 12 * k + hop * t, functools.partial(line_step, k, t)))
         for t in range(line):
             events.append((20 + period * k + 6 * t, functools.partial(plane_step, k, t)))
-        done = 30 + period * (k + 1)
+        done = 44 + period * (k + 1)
         events.append((done, functools.partial(arrived, k)))
         if k == 0:
             events.append((done, lambda: tokens_to_mate().wait_recv()))

time: 256 us -> 241 us (0.941)
  Pallas kernels: 245 us -> 229 us
    pallas_call x1, Pallas kernels: 245 us -> 229 us  [shards(): pl.pallas_call(functools.partial(kernel, groups, line, chunks), out_shape...]
where the time goes in v2:
time: 241 us
  Pallas kernels  229 us (95%)
  local copies, waits for them, and re-layouts  10.8 us (4%)
    pallas_call x1, Pallas kernels, shards(): pl.pallas_call(functools.partial(kernel, groups, line, chunks), out_shape...  229 us
    unnamed x10, local copies, waits for them, and re-layouts  10.8 us

profile of v2, /device:TPU:0, one launch (start us, length us, event | category | flops | bytes accessed | tf_op | source)
XLA Modules:
  0.0 240.7 jit_solution(6986319911870968561)
XLA Ops:
  0.6 229.2 %shard_map.93 = (f32[384,1536]{1,0:T(8,128)}, f32[384,1536]{1,0:T(8,128)}, bf16[512,3072]{1,0:T(8,128)(2,1)}, bf16[512,3072]{1,0:T(8,128)(2,1)}) custom-call(f32[1,384,6144]{2,1,0:T(8,128)} %student.1, bf16[512,3072]{1,0:T(8,128)(2,1)} %tokens.1, f32[384,1536]{1,0:T(8,128)} %teacher.1, f32[1,3072]{1,0:T(1,128)} %bitcast.3, f32[1,128]{1,0:T(1,128)} %bitcast.4, ...), custom_call_target="tpu_custom_call" | custom-call | flops 19327352832 | bytes 22020096 | tf_op jit(solution)/shard_map/pallas_call | solution.py:335
  229.9 0.0 copy-start.2
  229.9 3.4 %copy.14 = f32[384,1536]{1,0:T(8,128)} copy(f32[384,1536]{1,0:T(8,128)} %get-tuple-element.8) | data formatting | bytes 4718592
  233.3 0.0 copy-done.2
  233.3 0.0 copy-start.1
  233.3 1.4 copy.15
  234.7 1.3 copy-done.1
  236.0 0.0 copy-start
  236.0 1.7 copy.16
  237.7 1.4 copy-done
  239.0 1.7 copy.17
Async XLA Ops:
  229.9 3.4 %copy-start.2 = (f32[384,1536]{1,0:T(8,128)S(1)}, f32[384,1536]{1,0:T(8,128)}, u32[]{:S(2)}) copy-start(f32[384,1536]{1,0:T(8,128)} %get-tuple-element.9) | copy-start | bytes 7077892
  233.3 2.7 %copy-start.1 = (bf16[512,3072]{1,0:T(8,128)(2,1)S(1)}, bf16[512,3072]{1,0:T(8,128)(2,1)}, u32[]{:S(2)}) copy-start(bf16[512,3072]{1,0:T(8,128)(2,1)} %get-tuple-element.10) | copy-start | bytes 9437188
  236.0 3.0 %copy-start = (bf16[512,3072]{1,0:T(8,128)(2,1)S(1)}, bf16[512,3072]{1,0:T(8,128)(2,1)}, u32[]{:S(2)}) copy-start(bf16[512,3072]{1,0:T(8,128)(2,1)} %get-tuple-element.11) | copy-start | bytes 9437188

commit v3 on v2

--- a/solution.py
+++ b/solution.py
@@ -73,6 +73,8 @@
     below = (g, (z - 1) * PAIR + y)
     above = (g, (z + 1) * PAIR + y)
 
+    line_last = chunks - 1 if chunks > 2 else -1
+
     barrier = pltpu.get_barrier_semaphore()
     for device in (mate, across, beside):
         pl.semaphore_signal(barrier, inc=1, device_id=device, device_id_type=MESH)
@@ -119,7 +121,11 @@
         return weights.at[k, half, span, :]
 
     def along(k, slab, way):
-        part = shard(k, x, slab * PAIR + y)
+        if k == line_last:
+            span = pl.ds(pl.multiple_of(slab * PAIR * rows, 16), PAIR * rows)
+            part = weights.at[k, :, span, :]
+        else:
+            part = shard(k, x, slab * PAIR + y)
         return remote(
             part, part, line_send.at[k, way, slab], line_recv.at[k, slab], (below, above)[way]
         )
@@ -186,6 +192,18 @@
         pair_out[k] = (own_part[k, 1 - x] + core_part[k, 1 - x]).astype(jnp.bfloat16)
         to_across(k).start()
 
+    def line_start(k):
+        if k == line_last:
+            last(k, z).wait_recv()
+
+        @pl.when(z > 0)
+        def _():
+            along(k, z, 0).start()
+
+        @pl.when(z < line - 1)
+        def _():
+            along(k, z, 1).start()
+
     def sum_pair(k):
         to_across(k).wait_recv()
         total = (own_part[k, x] + core_part[k, x] + pair_in[k].astype(jnp.float32)) / groups
@@ -194,14 +212,8 @@
         teacher_out[k] = EMA_DECAY * teacher[:, here] + (1.0 - EMA_DECAY) * total
         weights[k, x, pl.ds(pl.multiple_of(f * rows, 16), rows), :] = total.astype(jnp.bfloat16)
 
-        @pl.when(z > 0)
-        def _():
-            along(k, z, 0).start()
-
-        @pl.when(z < line - 1)
-        def _():
-            along(k, z, 1).start()
-
+        if k != line_last:
+            line_start(k)
         first(k, z).start()
         for copy in stores(k):
             copy.start()
@@ -221,7 +233,8 @@
                 def _():
                     along(k, slab, way).start()
 
-                first(k, slab).start()
+                if k != line_last:
+                    first(k, slab).start()
 
     def plane_step(k, t):
         if t == 0:
@@ -282,12 +295,19 @@
     for k in range(chunks):
         events.append((4 + k, functools.partial(sum_cores, k)))
         events.append((12 + 4 * k, functools.partial(sum_pair, k)))
-        for t in range(1, line):
-            events.append((12 + 12 * k + hop * t, functools.partial(line_step, k, t)))
-        for t in range(line):
-            events.append((20 + period * k + 6 * t, functools.partial(plane_step, k, t)))
-        done = 44 + period * (k + 1)
-        events.append((done, functools.partial(arrived, k)))
+        if k == line_last:
+            events.append((18 + 4 * k, functools.partial(plane_step, k, 0)))
+            events.append((12 + 12 * k, functools.partial(line_start, k)))
+            for t in range(1, line):
+                events.append((12 + 12 * k + 20 * t, functools.partial(line_step, k, t)))
+            done = 33 + period * k
+        else:
+            for t in range(1, line):
+                events.append((12 + 12 * k + hop * t, functools.partial(line_step, k, t)))
+            for t in range(line):
+                events.append((20 + period * k + 6 * t, functools.partial(plane_step, k, t)))
+            done = 44 + period * (k + 1)
+            events.append((done, functools.partial(arrived, k)))
         if k == 0:
             events.append((done, lambda: tokens_to_mate().wait_recv()))
         for half in range(PAIR):
@@ -305,9 +325,13 @@
             give(k, half).wait_send()
         for copy in stores(k):
             copy.wait()
+        if k == line_last:
+            first(k, z).wait_send()
+            last(k, z).wait_send()
         for slab in range(line):
-            first(k, slab).wait_send()
-            last(k, slab).wait_send()
+            if k != line_last:
+                first(k, slab).wait_send()
+                last(k, slab).wait_send()
 
             @pl.when((z > 0) & (z <= slab))
             def _():

time: 241 us -> 244 us (1.012)
  no operation moved by 1% of the time
where the time goes in v3:
time: 244 us; the launch traced here: 243 us
  Pallas kernels  231 us (95%)
  local copies, waits for them, and re-layouts  10.8 us (4%)
    pallas_call x1, Pallas kernels, shards(): pl.pallas_call(functools.partial(kernel, groups, line, chunks), out_shape...  231 us
    unnamed x10, local copies, waits for them, and re-layouts  10.8 us

profile of v3, /device:TPU:0, one launch (start us, length us, event | category | flops | bytes accessed | tf_op | source)
XLA Modules:
  0.0 242.6 jit_solution(9849688106607857830)
XLA Ops:
  0.6 231.2 %shard_map.93 = (f32[384,1536]{1,0:T(8,128)}, f32[384,1536]{1,0:T(8,128)}, bf16[512,3072]{1,0:T(8,128)(2,1)}, bf16[512,3072]{1,0:T(8,128)(2,1)}) custom-call(f32[1,384,6144]{2,1,0:T(8,128)} %student.1, bf16[512,3072]{1,0:T(8,128)(2,1)} %tokens.1, f32[384,1536]{1,0:T(8,128)} %teacher.1, f32[1,3072]{1,0:T(1,128)} %bitcast.3, f32[1,128]{1,0:T(1,128)} %bitcast.4, ...), custom_call_target="tpu_custom_call" | custom-call | flops 19327352832 | bytes 22020096 | tf_op jit(solution)/shard_map/pallas_call | solution.py:359
  231.8 0.0 copy-start.2
  231.8 3.4 %copy.14 = f32[384,1536]{1,0:T(8,128)} copy(f32[384,1536]{1,0:T(8,128)} %get-tuple-element.8) | data formatting | bytes 4718592
  235.2 0.0 copy-done.2
  235.2 0.0 copy-start.1
  235.2 1.4 copy.15
  236.6 1.3 copy-done.1
  237.9 0.0 copy-start
  237.9 1.7 copy.16
  239.6 1.4 copy-done
  240.9 1.7 copy.17
Async XLA Ops:
  231.8 3.4 %copy-start.2 = (f32[384,1536]{1,0:T(8,128)S(1)}, f32[384,1536]{1,0:T(8,128)}, u32[]{:S(2)}) copy-start(f32[384,1536]{1,0:T(8,128)} %get-tuple-element.9) | copy-start | bytes 7077892
  235.2 2.7 %copy-start.1 = (bf16[512,3072]{1,0:T(8,128)(2,1)S(1)}, bf16[512,3072]{1,0:T(8,128)(2,1)}, u32[]{:S(2)}) copy-start(bf16[512,3072]{1,0:T(8,128)(2,1)} %get-tuple-element.10) | copy-start | bytes 9437188
  237.9 3.0 %copy-start = (bf16[512,3072]{1,0:T(8,128)(2,1)S(1)}, bf16[512,3072]{1,0:T(8,128)(2,1)}, u32[]{:S(2)}) copy-start(bf16[512,3072]{1,0:T(8,128)(2,1)} %get-tuple-element.11) | copy-start | bytes 9437188
